TPU v7x, 32 devices: a whole 2x2x4 slice. The times are simulated.
32 devices in a mesh: grp: 4 (over y, core), lon: 4 (over z), lat: 2 (over x).
Axes of the slice: x: 2, y: 2, z: 4, core: 2. Of those that a mesh axis runs over, the one named last changes fastest.
Arguments:
- state: float32 [4, 40, 96, 256], P('grp', None, 'lon', 'lat'), may hold values from -6 to 6
- depth: int32 [96, 256], P('lon', 'lat'), may hold values from 0 to 6
- rates: float32 [20, 20], replicated, may hold values from -1.25 to 1.25
- grazing: float32 [20], replicated, may hold values from -3 to 3
Outputs:
- state_out: float32 [4, 40, 96, 256], P('grp', None, 'lon', 'lat')
Inputs may be any that keep to these rules, and one draw needn't show every extreme that they name: `depth`: number of wet levels of a column; 0 is land.
All inputs are finite; a program needn't handle non-finite values.
Results may differ from a plain program's by a relative error of at most 0.0003.
Values sent between devices are 32-bit elements; how exact they have to be, the bound alone decides.
A program may use at most 64 MiB of HBM per device.

v0:
```python
import jax
import jax.numpy as jnp
from jax import lax
from jax.sharding import PartitionSpec as P

LZ = 2
NTR = 20
SECTIONS = 4
NSUB = 4


def padded_2(block, sides, width):
    for axis, dim in sides:
        count = lax.axis_size(axis)
        forward = [(i, i + 1) for i in range(count - 1)]
        forward.append((count - 1, 0))
        backward = [(target, source) for source, target in forward]
        low = lax.ppermute(
            lax.slice_in_dim(block, block.shape[dim] - width, None, axis=dim), axis, forward
        )
        high = lax.ppermute(lax.slice_in_dim(block, 0, width, axis=dim), axis, backward)
        block = jnp.concatenate([low, block, high], axis=dim)
    return block


def center_of(padded):
    return padded[..., 1:-1, 1:-1]


def grad_x(padded):
    return padded[..., 2:, 1:-1] - padded[..., :-2, 1:-1]


def grad_y(padded):
    return padded[..., 1:-1, 2:] - padded[..., 1:-1, :-2]


def laplace(padded):
    return (
        padded[..., 2:, 1:-1]
        + padded[..., :-2, 1:-1]
        + padded[..., 1:-1, 2:]
        + padded[..., 1:-1, :-2]
        - 4.0 * center_of(padded)
    )


def advance_dynamics(zonal_pad, merid_pad, temp_pad, surf_pad, wet_mask, land_mask, coriolis_rows):
    zonal = center_of(zonal_pad)
    merid = center_of(merid_pad)
    temper = center_of(temp_pad)
    surface = center_of(surf_pad)
    divergence = jnp.sum(grad_x(zonal_pad) + grad_y(merid_pad), axis=0)
    zonal_new = wet_mask * (zonal + coriolis_rows * merid - 0.5 * grad_x(surf_pad))
    merid_new = wet_mask * (merid - coriolis_rows * zonal - 0.5 * grad_y(surf_pad))
    surface_new = land_mask * (surface - 0.25 / zonal.shape[0] * divergence)
    temper_new = wet_mask * (
        temper
        - 0.25 * (zonal * grad_x(temp_pad) + merid * grad_y(temp_pad))
        + 0.1 * laplace(temp_pad)
    )
    return (zonal_new, merid_new, temper_new, surface_new)


def advect_tracers(tracer_pad, zonal, merid, wet_mask):
    return wet_mask * (
        center_of(tracer_pad)
        - 0.25 * (zonal * grad_x(tracer_pad) + merid * grad_y(tracer_pad))
        + 0.1 * laplace(tracer_pad)
    )


def section_rows(padded, wet_mask, land_mask, coriolis_rows):
    levels = (padded.shape[0] - 1) // 3
    results = advance_dynamics(
        padded[:levels],
        padded[levels : 2 * levels],
        padded[2 * levels : 3 * levels],
        padded[3 * levels],
        wet_mask,
        land_mask,
        coriolis_rows,
    )
    return jnp.concatenate([results[0], results[1], results[2], results[3][None]], axis=0)


def fix_rim(padded, width, lat_pos, lat_count):
    length = padded.shape[-1]
    positions = jnp.arange(length)
    lower = (positions < width) & (lat_pos == 0)
    upper = (positions >= length - width) & (lat_pos == lat_count - 1)
    return jnp.where(lower | upper, 0.0, padded)


def crop_rim(field, margin):
    return field[..., margin : field.shape[-2] - margin, margin : field.shape[-1] - margin]


def body(state, depth, rates, grazing):
    groups = lax.axis_size("grp")
    member = lax.axis_index("grp")
    lat_pos = lax.axis_index("lat")
    lat_count = lax.axis_size("lat")
    local = state[0]
    field_rows, columns, lat_rows = local.shape
    total_levels = LZ * (groups - 1)
    dyn_rows = 3 * total_levels + 1
    lat_total = lat_rows * lat_count
    depth_f = depth.astype(jnp.float32)
    level_index = jnp.arange(total_levels).astype(jnp.float32)[:, None, None]
    fields = local[:dyn_rows]
    bundle = jnp.concatenate([fields, depth_f[None]], axis=0)
    padded = padded_2(bundle, (("lon", 1), ("lat", 2)), SECTIONS)
    padded = fix_rim(padded, SECTIONS, lat_pos, lat_count)
    depth_pad = padded[-1]
    current = padded[:-1]
    wet_full = (level_index < depth_pad[None]).astype(jnp.float32)
    land_full = (depth_pad > 0).astype(jnp.float32)
    coord = (lat_pos * lat_rows - SECTIONS + jnp.arange(lat_rows + 2 * SECTIONS)).astype(
        jnp.float32
    )
    coriolis_full = 0.3 * jnp.sin(jnp.pi * (coord + 0.5) / lat_total - jnp.pi / 2)
    for section_index in range(SECTIONS):
        margin = section_index + 1
        current = section_rows(
            current,
            crop_rim(wet_full, margin),
            crop_rim(land_full, margin),
            coriolis_full[margin : coriolis_full.shape[0] - margin],
        )
    zonal = current[:total_levels]
    merid = current[total_levels : 2 * total_levels]
    temper = current[2 * total_levels : 3 * total_levels]
    surface = current[3 * total_levels]
    first_level = jnp.maximum(member - 1, 0) * LZ
    forcing = jnp.stack(
        [
            zonal.reshape(groups - 1, LZ, columns, lat_rows),
            merid.reshape(groups - 1, LZ, columns, lat_rows),
            temper.reshape(groups - 1, LZ, columns, lat_rows),
        ],
        axis=1,
    )
    outgoing = jnp.concatenate([jnp.zeros((1,) + forcing.shape[1:], jnp.float32), forcing], axis=0)
    received = lax.all_to_all(outgoing, "grp", split_axis=0, concat_axis=0, tiled=True)
    own_zonal = received[0, 0]
    own_merid = received[0, 1]
    own_temper = received[0, 2]
    member_levels = (first_level + jnp.arange(LZ)).astype(jnp.float32)[:, None, None]
    wet_member = (member_levels < depth_f[None]).astype(jnp.float32)
    bundle = jnp.concatenate([local, own_zonal, own_merid, depth_f[None]], axis=0)
    padded = padded_2(bundle, (("lon", 1), ("lat", 2)), NSUB)
    padded = fix_rim(padded, NSUB, lat_pos, lat_count)
    wide = columns + 2 * NSUB
    tall = lat_rows + 2 * NSUB
    advected = padded[:field_rows].reshape(NTR, LZ, wide, tall)
    zonal_pad = padded[field_rows : field_rows + LZ]
    merid_pad = padded[field_rows + LZ : field_rows + 2 * LZ]
    wet_pad = (member_levels < padded[-1][None]).astype(jnp.float32)
    for sub_index in range(NSUB):
        margin = sub_index + 1
        advected = advect_tracers(
            advected,
            crop_rim(zonal_pad, margin),
            crop_rim(merid_pad, margin),
            crop_rim(wet_pad, margin),
        )
    kinetic = jnp.einsum("ts,szxy->tzxy", rates, advected, precision=lax.Precision.HIGHEST)
    kinetic = kinetic + grazing[:, None, None, None] * (advected[0] * advected[1])[None]
    updated = wet_member[None] * (advected + 0.2 * jnp.exp(0.05 * own_temper)[None] * kinetic)
    light_factor = jnp.exp(-(member_levels + 0.5) / total_levels)
    heating = 0.3 * wet_member * updated[0] * light_factor
    returned = lax.all_gather(heating, "grp", axis=0, tiled=True)
    temper_final = temper + returned[LZ:]
    unused = jnp.zeros((field_rows - dyn_rows, columns, lat_rows), jnp.float32)
    dyn_out = jnp.concatenate([zonal, merid, temper_final, surface[None], unused], axis=0)
    result = jnp.where(member == 0, dyn_out, updated.reshape(field_rows, columns, lat_rows))
    return result[None]


def solution(mesh):
    in_specs = (P("grp", None, "lon", "lat"), P("lon", "lat"), P(), P())
    out_specs = P("grp", None, "lon", "lat")
    return jax.shard_map(body, mesh=mesh, in_specs=in_specs, out_specs=out_specs, check_vma=False)
```

profile of v0, /device:TPU:0, one launch (start us, length us, event | category | flops | bytes accessed | tf_op | source)
XLA Modules:
  0.0 73.4 jit_solution(11237631737677904527)
XLA Ops:
  0.0 0.7 fusion.41
  0.7 1.0 %slice_bitcast_fusion = f32[19,24,128]{2,1,0:T(8,128)S(1)} fusion(f32[1,40,24,128]{3,2,1,0:T(8,128)} %param.4), kind=kLoop, calls=%fused_computation.17 | loop fusion | bytes 466944 | tf_op jit(solution)/shard_map/slice | solution.py:111
  1.7 3.1 %collective-permute-start = (f32[20,4,128]{2,1,0:T(4,128)S(1)}, f32[20,4,128]{2,1,0:T(4,128)S(1)}, u32[]{:S(2)}, u32[]{:S(2)}) collective-permute-start(f32[20,4,128]{2,1,0:T(4,128)S(1)} %get-tuple-element.44), channel_id=1, source_target_pairs={{0,2},{2,4},{4,6},{6,0},{1,3},{3,5},{5,7},{7,1},{8,10},{10,12},{12... | collective-permute-start | bytes 122888 | tf_op jit(solution)/shard_map/ppermute | solution.py:18
  4.8 2.1 %collective-permute-start.1 = (f32[20,4,128]{2,1,0:T(4,128)S(1)}, f32[20,4,128]{2,1,0:T(4,128)S(1)}, u32[]{:S(2)}, u32[]{:S(2)}) collective-permute-start(f32[20,4,128]{2,1,0:T(4,128)S(1)} %get-tuple-element.45), channel_id=1, source_target_pairs={{2,0},{4,2},{6,4},{0,6},{3,1},{5,3},{7,5},{1,7},{10,8},{12,10},{14... | collective-permute-start | bytes 122888 | tf_op jit(solution)/shard_map/ppermute | solution.py:21
  6.9 2.0 %collective-permute-done = f32[20,4,128]{2,1,0:T(4,128)S(1)} collective-permute-done((f32[20,4,128]{2,1,0:T(4,128)S(1)}, f32[20,4,128]{2,1,0:T(4,128)S(1)}, u32[]{:S(2)}, u32[]{:S(2)}) %collective-permute-start) | collective-permute-done | bytes 40992 | tf_op jit(solution)/shard_map/ppermute | solution.py:18
  8.9 0.3 collective-permute-done.1
  9.3 0.2 fusion.40
  9.4 1.6 %collective-permute-start.2 = (f32[20,32,4]{2,1,0:T(8,128)S(1)}, f32[20,32,4]{2,1,0:T(8,128)S(1)}, u32[]{:S(2)}, u32[]{:S(2)}) collective-permute-start(f32[20,32,4]{2,1,0:T(8,128)S(1)} %get-tuple-element.39), channel_id=1, source_target_pairs={{0,1},{1,0},{2,3},{3,2},{4,5},{5,4},{6,7},{7,6},{8,9},{9,8},{10,11... | collective-permute-start | bytes 30728 | tf_op jit(solution)/shard_map/ppermute | solution.py:18
  11.0 0.5 collective-permute-start.3
  11.8 8.3 %collective-permute-done.2 = f32[20,32,4]{2,1,0:T(8,128)S(1)} collective-permute-done((f32[20,32,4]{2,1,0:T(8,128)S(1)}, f32[20,32,4]{2,1,0:T(8,128)S(1)}, u32[]{:S(2)}, u32[]{:S(2)}) %collective-permute-start.2) | collective-permute-done | bytes 10272 | tf_op jit(solution)/shard_map/ppermute | solution.py:18
  20.2 4.5 %collective-permute-done.3 = f32[20,32,4]{2,1,0:T(8,128)S(1)} collective-permute-done((f32[20,32,4]{2,1,0:T(8,128)S(1)}, f32[20,32,4]{2,1,0:T(8,128)S(1)}, u32[]{:S(2)}, u32[]{:S(2)}) %collective-permute-start.3) | collective-permute-done | bytes 10272 | tf_op jit(solution)/shard_map/ppermute | solution.py:21
  24.7 0.4 maximum_select_fusion.1
  25.1 0.2 fusion.9
  25.5 0.1 fusion.22
  25.6 0.4 subtract_multiply_fusion.5
  26.0 0.2 fusion.7
  26.2 0.1 fusion.19
  26.4 0.4 subtract_multiply_fusion.3
  26.8 0.2 fusion.5
  27.0 0.1 fusion.16
  27.2 0.4 subtract_multiply_fusion.1
  27.7 0.3 fusion.11
  27.9 0.1 bitcast_dynamic-update-slice_fusion.1
  28.1 0.1 bitcast_dynamic-update-slice_fusion
  28.2 0.7 select_maximum_fusion
  29.0 3.5 %all-to-all-start = ((f32[4,3,2,24,128]{4,3,2,1,0:T(8,128)}), f32[4,3,2,24,128]{4,3,2,1,0:T(8,128)S(1)}, u32[]{:S(2)}, u32[]{:S(2)}) async-start(f32[4,3,2,24,128]{4,3,2,1,0:T(8,128)} %select_maximum_fusion), calls=%async_computation | async-start | bytes 589824 | tf_op jit(solution)/shard_map/all_to_all | solution.py:145
  32.4 6.3 %all-to-all-done = f32[4,3,2,24,128]{4,3,2,1,0:T(8,128)S(1)} async-done(((f32[4,3,2,24,128]{4,3,2,1,0:T(8,128)}), f32[4,3,2,24,128]{4,3,2,1,0:T(8,128)S(1)}, u32[]{:S(2)}, u32[]{:S(2)}) %all-to-all-start) | async-done | bytes 294944 | tf_op jit(solution)/shard_map/all_to_all | solution.py:145
  38.8 1.2 %collective-permute-start.4 = (f32[45,4,128]{2,1,0:T(4,128)S(1)}, f32[45,4,128]{2,1,0:T(4,128)S(1)}, u32[]{:S(2)}, u32[]{:S(2)}) collective-permute-start(f32[45,4,128]{2,1,0:T(4,128)S(1)} %get-tuple-element.35), channel_id=1, source_target_pairs={{0,2},{2,4},{4,6},{6,0},{1,3},{3,5},{5,7},{7,1},{8,10},{10,12},{12... | collective-permute-start | bytes 276488 | tf_op jit(solution)/shard_map/ppermute | solution.py:18
  40.0 2.7 %collective-permute-start.5 = (f32[45,4,128]{2,1,0:T(4,128)S(1)}, f32[45,4,128]{2,1,0:T(4,128)S(1)}, u32[]{:S(2)}, u32[]{:S(2)}) collective-permute-start(f32[45,4,128]{2,1,0:T(4,128)S(1)} %get-tuple-element.36), channel_id=1, source_target_pairs={{2,0},{4,2},{6,4},{0,6},{3,1},{5,3},{7,5},{1,7},{10,8},{12,10},{14... | collective-permute-start | bytes 276488 | tf_op jit(solution)/shard_map/ppermute | solution.py:21
  42.8 3.2 %collective-permute-done.4 = f32[45,4,128]{2,1,0:T(4,128)S(1)} collective-permute-done((f32[45,4,128]{2,1,0:T(4,128)S(1)}, f32[45,4,128]{2,1,0:T(4,128)S(1)}, u32[]{:S(2)}, u32[]{:S(2)}) %collective-permute-start.4) | collective-permute-done | bytes 92192 | tf_op jit(solution)/shard_map/ppermute | solution.py:18
  46.0 0.1 pad_maximum_fusion
  46.2 0.3 fusion.39
  46.4 0.6 copy.17
  47.0 0.6 copy.18
  47.6 1.5 %collective-permute-start.7 = (f32[45,32,4]{0,1,2:T(8,128)S(1)}, f32[45,32,4]{0,1,2:T(8,128)S(1)}, u32[]{:S(2)}, u32[]{:S(2)}) collective-permute-start(f32[45,32,4]{0,1,2:T(8,128)S(1)} %copy.18), channel_id=1, source_target_pairs={{1,0},{0,1},{3,2},{2,3},{5,4},{4,5},{7,6},{6,7},{9,8},{8,9},{11,10... | collective-permute-start | bytes 69128 | tf_op jit(solution)/shard_map/ppermute | solution.py:21
  49.1 0.5 collective-permute-start.6
  49.6 3.7 %collective-permute-done.6 = f32[45,32,4]{0,1,2:T(8,128)S(1)} collective-permute-done((f32[45,32,4]{0,1,2:T(8,128)S(1)}, f32[45,32,4]{0,1,2:T(8,128)S(1)}, u32[]{:S(2)}, u32[]{:S(2)}) %collective-permute-start.6) | collective-permute-done | bytes 23072 | tf_op jit(solution)/shard_map/ppermute | solution.py:18
  53.4 0.7 copy.19
  54.1 0.7 copy.20
  54.8 0.9 %maximum_select_fusion = f32[45,32,136]{2,1,0:T(8,128)S(1)} fusion(f32[45,32,4]{2,1,0:T(8,128)S(1)} %copy.20, f32[45,4,128]{2,1,0:T(4,128)S(1)} %collective-permute-done.5, f32[1,24,128]{2,1,0:T(8,128)S(1)} %get-tuple-element.58, f32[2,24,128]{2,1,0:T(8,128)S(1)} %get-tuple-element.42, f32[2,24,128]{2,1,0:T(8,128)S(1)} %get-tuple-element.43, ...), kind=kLoop, calls=%fused_computation | loop fusion | flops 1566720 | bytes 1566856 | tf_op jit(solution)/shard_map/jit(_where)/select_n | solution.py:92
  56.6 1.5 %fusion.38 = (f32[20,2,30,134]{3,2,1,0:T(8,128)S(1)}, f32[20,2,30,134]{3,2,1,0:T(8,128)S(1)}, f32[20,2,30,134]{3,2,1,0:T(8,128)S(1)}, f32[20,2,30,134]{3,2,1,0:T(8,128)S(1)}, f32[20,2,30,134]{3,2,1,0:T(8,128)S(1)}) fusion(f32[20,2,32,136]{3,2,1,0:T(8,128)S(1)} %bitcast.56), kind=kLoop, calls=%fused_computation.112 | loop fusion | bytes 6432000 | tf_op jit(solution)/shard_map/slice | solution.py:31
  58.1 4.4 %add_multiply_fusion = f32[20,2,30,134]{3,0,2,1:T(8,128)S(1)} fusion(f32[20,2,30,134]{3,2,1,0:T(8,128)S(1)} %get-tuple-element.20, f32[20,2,30,134]{3,2,1,0:T(8,128)S(1)} %get-tuple-element.21, f32[20,2,30,134]{3,2,1,0:T(8,128)S(1)} %get-tuple-element.18, f32[20,2,30,134]{3,2,1,0:T(8,128)S(1)} %get-tuple-element.19, ...), kind=kLoop, calls=%fused_computation.1 | loop fusion | flops 2412000 | bytes 3955680 | tf_op jit(solution)/shard_map/mul | solution.py:66
  62.5 1.5 %add_multiply_fusion.1 = f32[20,2,28,132]{3,0,2,1:T(8,128)S(1)} fusion(f32[20,2,30,134]{3,0,2,1:T(8,128)S(1)} %add_multiply_fusion, f32[2,28,132]{2,1,0:T(8,128)S(1)} %get-tuple-element.14, f32[2,28,132]{2,1,0:T(8,128)S(1)} %get-tuple-element.13, f32[2,28,132]{2,1,0:T(8,128)S(1)} %slice.662), kind=kLoop, calls=%fused_computation.2 | loop fusion | flops 2217600 | bytes 3636864 | tf_op jit(solution)/shard_map/mul | solution.py:66
  64.0 1.4 %add_multiply_fusion.2 = f32[20,2,26,130]{3,0,2,1:T(8,128)S(1)} fusion(f32[20,2,28,132]{3,0,2,1:T(8,128)S(1)} %add_multiply_fusion.1, f32[2,26,130]{2,1,0:T(8,128)S(1)} %get-tuple-element.12, f32[2,26,130]{2,1,0:T(8,128)S(1)} %get-tuple-element.11, f32[2,26,130]{2,1,0:T(8,128)S(1)} %slice.661), kind=kLoop, calls=%fused_computation.3 | loop fusion | flops 2028000 | bytes 3325920 | tf_op jit(solution)/shard_map/mul | solution.py:66
  65.4 0.7 add_multiply_fusion.3
  66.2 0.7 fusion.3
  67.1 5.3 %all_gather.3 = f32[8,24,128]{2,1,0:T(8,128)S(1)} all-gather(f32[2,24,128]{2,1,0:T(8,128)S(1)} %fusion.24), channel_id=1, replica_groups=mesh['grp'=4,'lon'=4,'lat'=2] {'grp'}, dimensions={0}, use_global_device_ids=true | all-gather | bytes 122880 | tf_op jit(solution)/shard_map/all_gather | solution.py:173
  72.6 0.8 %bitcast_select_fusion = f32[1,40,24,128]{3,2,1,0:T(8,128)} fusion(f32[1,40,24,128]{3,2,1,0:T(8,128)S(1)} %broadcast_dynamic-update-slice_fusion, pred[]{:T(512)S(6)} %eq.11, f32[1,40,24,128]{3,2,1,0:T(8,128)S(1)} %bitcast.60), kind=kLoop, calls=%fused_computation.12 | loop fusion | flops 122880 | bytes 1474561 | tf_op jit(solution)/shard_map/jit(_where)/select_n | solution.py:177
  (44 shorter events, 1.9 us)
Async XLA Ops:
  0.0 66.2 %copy-start = (f32[20,20]{1,0:T(8,128)S(1)}, f32[20,20]{1,0:T(8,128)}, u32[]{:S(2)}) copy-start(f32[20,20]{1,0:T(8,128)} %param.6) | copy-start | bytes 4804
  1.7 7.2 %collective-permute-start = (f32[20,4,128]{2,1,0:T(4,128)S(1)}, f32[20,4,128]{2,1,0:T(4,128)S(1)}, u32[]{:S(2)}, u32[]{:S(2)}) collective-permute-start(f32[20,4,128]{2,1,0:T(4,128)S(1)} %get-tuple-element.44), channel_id=1, source_target_pairs={{0,2},{2,4},{4,6},{6,0},{1,3},{3,5},{5,7},{7,1},{8,10},{10,12},{12... | collective-permute-start | bytes 122888 | tf_op jit(solution)/shard_map/ppermute | solution.py:18
  4.8 4.4 %collective-permute-start.1 = (f32[20,4,128]{2,1,0:T(4,128)S(1)}, f32[20,4,128]{2,1,0:T(4,128)S(1)}, u32[]{:S(2)}, u32[]{:S(2)}) collective-permute-start(f32[20,4,128]{2,1,0:T(4,128)S(1)} %get-tuple-element.45), channel_id=1, source_target_pairs={{2,0},{4,2},{6,4},{0,6},{3,1},{5,3},{7,5},{1,7},{10,8},{12,10},{14... | collective-permute-start | bytes 122888 | tf_op jit(solution)/shard_map/ppermute | solution.py:21
  9.4 10.7 %collective-permute-start.2 = (f32[20,32,4]{2,1,0:T(8,128)S(1)}, f32[20,32,4]{2,1,0:T(8,128)S(1)}, u32[]{:S(2)}, u32[]{:S(2)}) collective-permute-start(f32[20,32,4]{2,1,0:T(8,128)S(1)} %get-tuple-element.39), channel_id=1, source_target_pairs={{0,1},{1,0},{2,3},{3,2},{4,5},{5,4},{6,7},{7,6},{8,9},{9,8},{10,11... | collective-permute-start | bytes 30728 | tf_op jit(solution)/shard_map/ppermute | solution.py:18
  11.0 13.7 %collective-permute-start.3 = (f32[20,32,4]{2,1,0:T(8,128)S(1)}, f32[20,32,4]{2,1,0:T(8,128)S(1)}, u32[]{:S(2)}, u32[]{:S(2)}) collective-permute-start(f32[20,32,4]{2,1,0:T(8,128)S(1)} %get-tuple-element.40), channel_id=1, source_target_pairs={{1,0},{0,1},{3,2},{2,3},{5,4},{4,5},{7,6},{6,7},{9,8},{8,9},{11,10... | collective-permute-start | bytes 30728 | tf_op jit(solution)/shard_map/ppermute | solution.py:21
  27.7 11.1 %copy-start.1 = (f32[1,40,24,128]{3,2,1,0:T(8,128)S(1)}, f32[1,40,24,128]{3,2,1,0:T(8,128)}, u32[]{:S(2)}) copy-start(f32[1,40,24,128]{3,2,1,0:T(8,128)} %param.4) | copy-start | bytes 1474564
  29.0 9.8 %all-to-all-start = ((f32[4,3,2,24,128]{4,3,2,1,0:T(8,128)}), f32[4,3,2,24,128]{4,3,2,1,0:T(8,128)S(1)}, u32[]{:S(2)}, u32[]{:S(2)}) async-start(f32[4,3,2,24,128]{4,3,2,1,0:T(8,128)} %select_maximum_fusion), calls=%async_computation | async-start | bytes 589824 | tf_op jit(solution)/shard_map/all_to_all | solution.py:145
  38.8 7.2 %collective-permute-start.4 = (f32[45,4,128]{2,1,0:T(4,128)S(1)}, f32[45,4,128]{2,1,0:T(4,128)S(1)}, u32[]{:S(2)}, u32[]{:S(2)}) collective-permute-start(f32[45,4,128]{2,1,0:T(4,128)S(1)} %get-tuple-element.35), channel_id=1, source_target_pairs={{0,2},{2,4},{4,6},{6,0},{1,3},{3,5},{5,7},{7,1},{8,10},{10,12},{12... | collective-permute-start | bytes 276488 | tf_op jit(solution)/shard_map/ppermute | solution.py:18
  40.0 6.0 %collective-permute-start.5 = (f32[45,4,128]{2,1,0:T(4,128)S(1)}, f32[45,4,128]{2,1,0:T(4,128)S(1)}, u32[]{:S(2)}, u32[]{:S(2)}) collective-permute-start(f32[45,4,128]{2,1,0:T(4,128)S(1)} %get-tuple-element.36), channel_id=1, source_target_pairs={{2,0},{4,2},{6,4},{0,6},{3,1},{5,3},{7,5},{1,7},{10,8},{12,10},{14... | collective-permute-start | bytes 276488 | tf_op jit(solution)/shard_map/ppermute | solution.py:21
  47.6 6.5 %collective-permute-start.7 = (f32[45,32,4]{0,1,2:T(8,128)S(1)}, f32[45,32,4]{0,1,2:T(8,128)S(1)}, u32[]{:S(2)}, u32[]{:S(2)}) collective-permute-start(f32[45,32,4]{0,1,2:T(8,128)S(1)} %copy.18), channel_id=1, source_target_pairs={{1,0},{0,1},{3,2},{2,3},{5,4},{4,5},{7,6},{6,7},{9,8},{8,9},{11,10... | collective-permute-start | bytes 69128 | tf_op jit(solution)/shard_map/ppermute | solution.py:21
  49.1 4.3 %collective-permute-start.6 = (f32[45,32,4]{0,1,2:T(8,128)S(1)}, f32[45,32,4]{0,1,2:T(8,128)S(1)}, u32[]{:S(2)}, u32[]{:S(2)}) collective-permute-start(f32[45,32,4]{0,1,2:T(8,128)S(1)} %copy.17), channel_id=1, source_target_pairs={{0,1},{1,0},{2,3},{3,2},{4,5},{5,4},{6,7},{7,6},{8,9},{9,8},{10,11... | collective-permute-start | bytes 69128 | tf_op jit(solution)/shard_map/ppermute | solution.py:18
  65.4 0.8 %copy-start.2 = (f32[20]{0:T(128)S(1)}, f32[20]{0:T(128)}, u32[]{:S(2)}) copy-start(f32[20]{0:T(128)} %param.7) | copy-start | bytes 244
where the time goes:
time: 73.7 us; the launch traced here: 73.4 us
  waiting for transfers between devices  28.4 us (39%)
  starting transfers between devices  16.7 us (23%)
  other arithmetic  15.2 us (21%)
  local copies, waits for them, and re-layouts  6.67 us (9%)
  blocking collectives  5.32 us (7%)
    ppermute x4, waiting for transfers between devices, padded_2(): lax.ppermute(lax.slice_in_dim(block, block.shape[dim] - width, None, axis...  17.2 us
    mul x4, other arithmetic, advect_tracers(): wet_mask * (center_of(tracer_pad) - 0.25 * (zonal * grad_x(tracer_pad) +...  7.98 us
    ppermute x4, starting transfers between devices, padded_2(): lax.ppermute(lax.slice_in_dim(block, 0, width, axis=dim), axis, backward)  6.87 us
    ppermute x4, starting transfers between devices, padded_2(): lax.ppermute(lax.slice_in_dim(block, block.shape[dim] - width, None, axis...  6.36 us
    all_to_all x1, waiting for transfers between devices, body(): lax.all_to_all(outgoing, 'grp', split_axis=0, concat_axis=0, tiled=True)  6.33 us
    all_gather x1, blocking collectives, body(): returned = lax.all_gather(heating, 'grp', axis=0, tiled=True)  5.32 us
    ppermute x4, waiting for transfers between devices, padded_2(): lax.ppermute(lax.slice_in_dim(block, 0, width, axis=dim), axis, backward)  4.85 us
    all_to_all x1, starting transfers between devices, body(): lax.all_to_all(outgoing, 'grp', split_axis=0, concat_axis=0, tiled=True)  3.45 us
  transfers between devices with their start and end apart: 9, of which 7 were waited for; matrix products, arithmetic and copies ran while one was open for 2% of the time, Pallas kernels for 0%

commit v1 on v0

v1 whole, which is shorter than its diff:
```python
import functools

import jax
import jax.numpy as jnp
from jax import lax
from jax.experimental import pallas as pl
from jax.experimental.pallas import tpu as pltpu
from jax.sharding import PartitionSpec as P

LZ = 2
NTR = 20
SECTIONS = 4
NSUB = 4
HD = SECTIONS + NSUB - 1
HT = NSUB
HV = NSUB - 1
WD = HD + 11
MESH = pl.DeviceIdType.MESH
F32 = jnp.float32


def roll(a, shift, axis=None):
    axis = a.ndim - 1 if axis is None else axis
    shift = shift % a.shape[axis]
    return a if shift == 0 else pltpu.roll(a, shift, axis)


def each(count, step):
    def one(i, carry):
        step(i)
        return carry

    lax.fori_loop(0, count, one, 0, unroll=True)


def kernel(
    groups, lons, lats,
    state, depth, rates, grazing, out,
    dyn_a, dyn_b, wet_d, land_d, edge, low, high, pack_core, pack_strip,
    got_core, got_strip, tr_a, tr_b, st_a, st_b, coef, coef_s, extra, theta_send, theta_got,
    send_sem, recv_sem, pack_send, pack_recv, back_send, back_recv,
):
    nx, ny = depth.shape
    levels = LZ * (groups - 1)
    tiles = state.shape[0] // nx // 8
    member = lax.axis_index("grp")
    lon = lax.axis_index("lon")
    lat = lax.axis_index("lat")
    has_low = lat > 0
    has_high = lat < lats - 1
    lane = lax.broadcasted_iota(jnp.int32, (8, ny), 1)
    sub = lax.broadcasted_iota(jnp.int32, (8, ny), 0)
    half = lane % 64
    is_low = lane < 64

    def peer(dx, dy):
        return (member, (lon + dx + lons) % lons, lat + dy)

    barrier = pltpu.get_barrier_semaphore()

    def signal(device):
        pl.semaphore_signal(barrier, inc=1, device_id=device, device_id_type=MESH)

    for dx in (-1, 1):
        signal(peer(dx, 0))

    @pl.when(has_low)
    def _():
        for dx in (-1, 0, 1):
            signal(peer(dx, -1))

    @pl.when(has_high)
    def _():
        for dx in (-1, 0, 1):
            signal(peer(dx, 1))

    @pl.when(member == 0)
    def _():
        for m in range(1, groups):
            signal((m, lon, lat))

    @pl.when(member != 0)
    def _():
        signal((0, lon, lat))

    @pl.when(lat == 0)
    def _():
        low[...] = jnp.zeros(low.shape, F32)

    @pl.when(lat == lats - 1)
    def _():
        high[...] = jnp.zeros(high.shape, F32)

    def barrier_wait():
        beside = has_low.astype(jnp.int32) + has_high.astype(jnp.int32)
        pl.semaphore_wait(barrier, 2 + 3 * beside + jnp.where(member == 0, groups - 1, 1))

    def exchange(core, h):
        copies = []
        for dy in (0, -1, 1):
            for dx in (-1, 0, 1):
                if dx == 0 and dy == 0:
                    continue
                start = nx - h if dx == 1 else 0
                size = h if dx else nx
                to = {1: 0, 0: h, -1: h + nx}[dx]
                if dy == 0:
                    src = core(h + start, size)
                    dst = core(to, size)
                else:
                    src = edge.at[pl.ds(start, size)]
                    dst = (low if dy == 1 else high).at[pl.ds(to, size)]
                index = (dy + 1) * 3 + dx + 1
                copy = pltpu.make_async_remote_copy(
                    src_ref=src, dst_ref=dst,
                    send_sem=send_sem.at[index], recv_sem=recv_sem.at[index],
                    device_id=peer(dx, dy), device_id_type=MESH,
                )
                copies.append((dy, copy))

        def guarded(there, action):
            if there is None:
                action()
            else:
                pl.when(there)(action)

        sends = {0: None, -1: has_low, 1: has_high}
        comes = {0: None, -1: has_high, 1: has_low}

        def start():
            for dy, copy in copies:
                guarded(sends[dy], copy.start)

        def arrived():
            for dy, copy in copies:
                guarded(comes[dy], copy.wait_recv)

        def left():
            for dy, copy in copies:
                guarded(sends[dy], copy.wait_send)

        return start, arrived, left

    def pack_copies(m):
        pairs = ((pack_core, got_core), (pack_strip, got_strip))
        return [
            pltpu.make_async_remote_copy(
                src_ref=src.at[m - 1], dst_ref=dst,
                send_sem=pack_send.at[m - 1, i], recv_sem=pack_recv.at[i],
                device_id=(m, lon, lat), device_id_type=MESH,
            )
            for i, (src, dst) in enumerate(pairs)
        ]

    def back_copy(m):
        return pltpu.make_async_remote_copy(
            src_ref=theta_send, dst_ref=theta_got.at[m - 1],
            send_sem=back_send, recv_sem=back_recv.at[m - 1],
            device_id=(0, lon, lat), device_id_type=MESH,
        )

    @pl.when(member == 0)
    def _():
        def load(x):
            dep = jnp.broadcast_to(depth[pl.ds(x, 1), :].astype(F32), (8, ny))
            eta = jnp.broadcast_to(state[pl.ds(3 * levels * nx + x, 1), :], (8, ny))
            fields = [
                jnp.where(sub < levels, state[pl.ds(q * levels * nx + x, 8, stride=nx), :], 0.0)
                for q in range(3)
            ]
            fields.append(jnp.where(sub < 4, eta, dep))
            packet = jnp.zeros((8, ny), F32)
            for q in range(4):
                dyn_a[HD + x, 0, q] = fields[q]
                near = jnp.where(is_low, roll(fields[q], HD + HD * q), roll(fields[q], 75 + HD * q))
                begin = jnp.where(is_low, HD * q, 75 + HD * q)
                packet = jnp.where((lane >= begin) & (lane < begin + HD), near, packet)
            edge[x] = packet

        each(nx, load)
        start, arrived, left = exchange(lambda at, size: dyn_a.at[pl.ds(at, size), 0], HD)
        barrier_wait()
        start()
        arrived()
        left()

        level = sub.astype(F32)

        def unpack(r):
            from_low = low[r]
            from_high = high[r]
            for q in range(4):
                field = dyn_a[r, 0, q]
                strip = jnp.where(is_low, roll(field, HD), roll(field, 75))
                strip = jnp.where(lane < HD, roll(from_low, -HD * q), strip)
                strip = jnp.where((lane >= 75) & (lane < 75 + HD), roll(from_high, -HD * q), strip)
                if q < 3:
                    dyn_a[r, 1, q] = strip
                else:
                    for i, both in enumerate((field, strip)):
                        dyn_a[r, i, 3] = jnp.broadcast_to(both[0:1], (8, ny))
                        dep = jnp.broadcast_to(both[4:5], (8, ny))
                        wet_d[r, i] = (level < dep).astype(F32)
                        land_d[r, i] = dep

        each(nx + 2 * HD, unpack)

        def rows_of(lat_index):
            return 0.3 * jnp.sin(jnp.pi * (lat_index.astype(F32) + 0.5) / (lats * ny) - jnp.pi / 2)

        base = lat * ny
        strip_y = jnp.where(is_low, lane - HD, lane - 64 + ny - 11)
        cor = jnp.stack([rows_of(base + lane), rows_of(base + strip_y)])
        current, following = dyn_a, dyn_b
        for section in range(SECTIONS):
            def advance(i, section=section, current=current, following=following):
                r = i + section + 1
                u, v, th, eta = (current[r, :, q] for q in range(4))
                up, tp, ep = (current[r + 1, :, q] for q in (0, 2, 3))
                um, tm, em = (current[r - 1, :, q] for q in (0, 2, 3))
                vyp, vym = roll(v, -1), roll(v, 1)
                typ, tym = roll(th, -1), roll(th, 1)
                eyp, eym = roll(eta, -1), roll(eta, 1)
                wet = wet_d[r]
                div = jnp.sum((up - um) + (vyp - vym), axis=1, keepdims=True)
                new_eta = eta - (0.25 / levels) * div
                results = (
                    wet * (u + cor * v - 0.5 * (ep - em)),
                    wet * (v - cor * u - 0.5 * (eyp - eym)),
                    wet * (
                        th - 0.25 * (u * (tp - tm) + v * (typ - tym))
                        + 0.1 * (((tp + tm) + (typ + tym)) - 4.0 * th)
                    ),
                    jnp.where(land_d[r] > 0, new_eta, 0.0),
                )
                for q, new in enumerate(results):
                    if section < SECTIONS - 1:
                        following[r, :, q] = new
                    else:
                        core = jnp.where(lane < 4, roll(new[1], -HD), new[0])
                        core = jnp.where(lane >= ny - 4, roll(new[1], ny - 4 - 64 - HD), core)
                        following[r, 0, q] = core
                        following[r, 1, q] = new[1]

            each(nx + 2 * HD - 2 * (section + 1), advance)
            current, following = following, current

        def bundle(i):
            strips = [None] * (groups - 1)
            for part in range(3):
                r = SECTIONS + 3 * i + part
                u, v, th = (current[r, :, q] for q in range(3))
                dep = land_d[r]
                for m in range(groups - 1):
                    both = jnp.where(sub < 6, roll(th, 4 - LZ * m, 1), dep)
                    both = jnp.where(sub < 4, roll(v, 2 - LZ * m, 1), both)
                    both = jnp.where(sub < 2, roll(u, -LZ * m, 1), both)
                    pack_core[m, 3 * i + part] = both[0]
                    moved = roll(both[1], WD * part)
                    if part == 0:
                        strips[m] = moved
                    else:
                        strips[m] = jnp.where(half >= WD * part, moved, strips[m])
            for m in range(groups - 1):
                pack_strip[m, i] = strips[m]

        each((nx + 2 * HV) // 3, bundle)
        for m in range(1, groups):
            for copy in pack_copies(m):
                copy.start()

        def emit(x):
            for q in range(2):
                out[pl.ds(q * levels * nx + x, levels, stride=nx), :] = current[HD + x, 0, q][:levels]
            out[pl.ds(3 * levels * nx + x, 1), :] = current[HD + x, 0, 3][0:1]

        each(nx, emit)
        used = (3 * levels + 1) * nx
        out[used:, :] = jnp.zeros((out.shape[0] - used, ny), F32)
        for m in range(1, groups):
            for copy in pack_copies(m):
                copy.wait_send()
        for m in range(1, groups):
            back_copy(m).wait_recv()
        for m in range(1, groups):
            at = (2 * levels + LZ * (m - 1)) * nx
            out[at : at + LZ * nx, :] = theta_got[m - 1]

    @pl.when(member != 0)
    def _():
        place = half % 12
        slot = half // 12

        def load(x):
            near = jnp.zeros((8, ny), F32)
            for j in range(tiles):
                tile = state[pl.ds(8 * j * nx + x, 8, stride=nx), :]
                tr_a[HT + x, j] = tile
                moved = jnp.where(is_low, roll(tile, 12 * j + 4), roll(tile, 12 * j + 72))
                near = jnp.where(slot == j, moved, near)
            edge[x] = near

        each(nx, load)
        start, arrived, left = exchange(lambda at, size: tr_a.at[pl.ds(at, size)], HT)
        barrier_wait()
        start()

        rows = LZ * NTR
        spread = (
            lax.broadcasted_iota(jnp.int32, (rows, NTR), 0) // LZ
            == lax.broadcasted_iota(jnp.int32, (rows, NTR), 1)
        ).astype(F32)
        spread_t = (
            lax.broadcasted_iota(jnp.int32, (NTR, rows), 1) // LZ
            == lax.broadcasted_iota(jnp.int32, (NTR, rows), 0)
        ).astype(F32)
        exact = dict(precision=lax.Precision.HIGHEST, preferred_element_type=F32)
        wide = jnp.dot(jnp.dot(spread, rates[...], **exact), spread_t, **exact)
        same = (
            lax.broadcasted_iota(jnp.int32, (rows, rows), 0) % LZ
            == lax.broadcasted_iota(jnp.int32, (rows, rows), 1) % LZ
        )
        wide = jnp.where(same, wide, 0.0)
        wide_hi = wide.astype(jnp.bfloat16).astype(F32)
        wide_lo = wide - wide_hi
        mixing = jnp.concatenate([wide_hi, wide_hi, wide_lo], axis=1)
        graze = jnp.sum(spread * grazing[...], axis=1, keepdims=True)
        graze = jnp.broadcast_to(graze, (rows, ny)).reshape(tiles, 8, ny)

        arrived()
        left()

        def join(r):
            near = jnp.zeros((8, ny), F32)
            for j in range(tiles):
                tile = tr_a[r, j]
                moved = jnp.where(is_low, roll(tile, 12 * j + 4), roll(tile, 12 * j + 72))
                near = jnp.where(slot == j, moved, near)
            near = jnp.where(is_low & (place < 4), low[r], near)
            near = jnp.where((lane >= 64) & (place >= 8), high[r], near)
            st_a[r] = near

        each(nx + 2 * HT, join)

        first = LZ * (member - 1)
        odd = sub % LZ
        level = (first + odd).astype(F32)
        for copy in pack_copies(1):
            copy.wait_recv()

        def pattern(v, i):
            return jnp.where(odd == 0, v[i : i + 1], v[i + 1 : i + 2])

        def factors(packet, target, r):
            u = pattern(packet, 0)
            v = pattern(packet, 2)
            wet = (level < packet[6:7]).astype(F32)
            target[r, 0] = 0.6 * wet
            for i, value in enumerate((u, v)):
                target[r, 2 * i + 1] = wet * (0.1 - 0.25 * value)
                target[r, 2 * i + 2] = wet * (0.1 + 0.25 * value)
            return wet

        def coefficients(i):
            strip = got_strip[i]
            for part in range(3):
                r = 3 * i + part
                packet = got_core[r]
                wet = factors(packet, coef, r)
                extra[r, 0] = wet
                extra[r, 1] = pattern(packet, 4)
                spread_strip = roll(strip, -3 - WD * part)
                for j in range(1, tiles):
                    moved = roll(strip, 12 * j - 3 - WD * part)
                    spread_strip = jnp.where(slot == j, moved, spread_strip)
                factors(spread_strip, coef_s, r)

        each((nx + 2 * HV) // 3, coefficients)

        cur, nxt, cur_s, nxt_s = tr_a, tr_b, st_a, st_b
        for step in range(NSUB):
            def advance(i, step=step, cur=cur, nxt=nxt, cur_s=cur_s, nxt_s=nxt_s):
                r = i + step + 1
                a, xp, xm, yp, ym = (coef[r - 1, k] for k in range(5))
                for j in range(tiles):
                    c = cur[r, j]
                    nxt[r, j] = (a * c + (xp * cur[r + 1, j] + xm * cur[r - 1, j])) + (
                        yp * roll(c, -1) + ym * roll(c, 1)
                    )
                a, xp, xm, yp, ym = (coef_s[r - 1, k] for k in range(5))
                c = cur_s[r]
                nxt_s[r] = (a * c + (xp * cur_s[r + 1] + xm * cur_s[r - 1])) + (
                    yp * roll(c, -1) + ym * roll(c, 1)
                )

            each(nx + 2 * HT - 2 * (step + 1), advance)
            cur, nxt, cur_s, nxt_s = nxt, cur, nxt_s, cur_s

        light = 0.3 * jnp.exp(-(level + 0.5) / levels)

        def react(x):
            strip = cur_s[HT + x]
            parts = []
            for j in range(tiles):
                c = cur[HT + x, j]
                c = jnp.where(lane < 4, roll(strip, -12 * j - 4), c)
                parts.append(jnp.where(lane >= ny - 4, roll(strip, 56 - 12 * j), c))
            c = jnp.concatenate(parts, axis=0)
            c_hi = c.astype(jnp.bfloat16).astype(F32)
            stacked = jnp.concatenate([c_hi, c - c_hi, c_hi], axis=0)
            kinetic = jnp.dot(mixing, stacked, preferred_element_type=F32)
            product = parts[0] * roll(parts[0], -LZ, 0)
            product = pattern(product, 0)
            wet = extra[HV + x, 0]
            th = extra[HV + x, 1]
            growth = 0.2 * jnp.exp(0.05 * th)
            for j in range(tiles):
                both = kinetic[8 * j : 8 * j + 8] + graze[j] * product
                new = wet * (parts[j] + growth * both)
                out[pl.ds(8 * j * nx + x, 8, stride=nx), :] = new
                if j == 0:
                    final = th + light * wet * new
                    theta_send[pl.ds(x, LZ, stride=nx), :] = final[:LZ]

        each(nx, react)
        back = back_copy(member)
        back.start()
        back.wait_send()


def solution(mesh):
    groups, lons, lats = (mesh.shape[a] for a in ("grp", "lon", "lat"))

    def body(state, depth, rates, grazing):
        _, planes, nx, ny = state.shape
        tiles = planes // 8
        xd, xt, xv = nx + 2 * HD, nx + 2 * HT, nx + 2 * HV
        vmem = lambda *shape: pltpu.VMEM(shape, F32)
        dma = pltpu.SemaphoreType.DMA
        flat = pl.pallas_call(
            functools.partial(kernel, groups, lons, lats),
            out_shape=jax.ShapeDtypeStruct((planes * nx, ny), F32),
            in_specs=[pl.BlockSpec(memory_space=pltpu.VMEM)] * 4,
            out_specs=pl.BlockSpec(memory_space=pltpu.VMEM),
            scratch_shapes=[
                vmem(xd, 2, 4, 8, ny), vmem(xd, 2, 4, 8, ny),
                vmem(xd, 2, 8, ny), vmem(xd, 2, 8, ny),
                vmem(nx, 8, ny), vmem(xd, 8, ny), vmem(xd, 8, ny),
                vmem(groups - 1, xv, 8, ny), vmem(groups - 1, xv // 3, 8, ny),
                vmem(xv, 8, ny), vmem(xv // 3, 8, ny),
                vmem(xt, tiles, 8, ny), vmem(xt, tiles, 8, ny),
                vmem(xt, 8, ny), vmem(xt, 8, ny),
                vmem(xv, 5, 8, ny), vmem(xv, 5, 8, ny), vmem(xv, 2, 8, ny),
                vmem(LZ * nx, ny), vmem(groups - 1, LZ * nx, ny),
                dma((9,)), dma((9,)), dma((groups - 1, 2)), dma((2,)), dma, dma((groups - 1,)),
            ],
            compiler_params=pltpu.CompilerParams(
                collective_id=0, has_side_effects=True, vmem_limit_bytes=40 * 2**20
            ),
            cost_estimate=pl.CostEstimate(
                flops=40_000_000, bytes_accessed=8 * planes * nx * ny, transcendentals=8192
            ),
        )(state.reshape(planes * nx, ny), depth, rates, grazing.reshape(1, NTR))
        return flat.reshape(state.shape)

    return jax.shard_map(
        body, mesh=mesh,
        in_specs=(P("grp", None, "lon", "lat"), P("lon", "lat"), P(), P()),
        out_specs=P("grp", None, "lon", "lat"), check_vma=False,
    )
```

time: 73.7 us -> 31.7 us (0.43)
  waiting for transfers between devices: 28.4 us -> 0 us
  Pallas kernels: 0 us -> 27.5 us
  starting transfers between devices: 16.7 us -> 0 us
  other arithmetic: 15.2 us -> 0 us
  blocking collectives: 5.32 us -> 0 us
  local copies, waits for them, and re-layouts: 6.67 us -> 3.88 us
    pallas_call x0 -> x1, Pallas kernels: none -> 27.5 us  [body(): pl.pallas_call(functools.partial(kernel, groups, lons, lats), out_shape=j...]
    ppermute x8 -> x0, waiting for transfers between devices: 22.1 us -> none  [the longest x4 17.2 us: padded_2(): lax.ppermute(lax.slice_in_dim(block, block.shape[dim] - width, None, axis...]
    ppermute x8 -> x0, starting transfers between devices: 13.2 us -> none  [the longest x4 6.87 us: padded_2(): lax.ppermute(lax.slice_in_dim(block, 0, width, axis=dim), axis, backward)]
    mul x15 -> x0, other arithmetic: 9.85 us -> none  [the longest x4 7.98 us: advect_tracers(): wet_mask * (center_of(tracer_pad) - 0.25 * (zonal * grad_x(tracer_pad) +...]
    all_to_all x1 -> x0, waiting for transfers between devices: 6.33 us -> none  [body(): lax.all_to_all(outgoing, 'grp', split_axis=0, concat_axis=0, tiled=True)]
    all_gather x1 -> x0, blocking collectives: 5.32 us -> none  [body(): returned = lax.all_gather(heating, 'grp', axis=0, tiled=True)]
    slice x20 -> x0, local copies, waits for them, and re-layouts: 5.09 us -> none  [the longest x1 1.5 us: grad_x(): return padded[..., 2:, 1:-1] - padded[..., :-2, 1:-1]]
    unnamed x6 -> x9, local copies, waits for them, and re-layouts: 0.02 us -> 3.88 us
  transfers between devices with their start and end apart: 9 -> 0, of which waited for: 7 -> 0; matrix products, arithmetic and copies ran while one was open for 2% -> 0% of each run, Pallas kernels for 0% -> 0%
where the time goes in v1:
time: 31.7 us; the launch traced here: 31.4 us
  Pallas kernels  27.5 us (87%)
  local copies, waits for them, and re-layouts  3.88 us (12%)
    pallas_call x1, Pallas kernels, body(): pl.pallas_call(functools.partial(kernel, groups, lons, lats), out_shape=j...  27.5 us
    unnamed x9, local copies, waits for them, and re-layouts  3.88 us

profile of v1, /device:TPU:0, one launch (start us, length us, event | category | flops | bytes accessed | tf_op | source)
XLA Modules:
  0.0 31.4 jit_solution(11983747026133606635)
XLA Ops:
  0.0 0.0 copy-start.3
  0.0 0.7 %copy-done.3 = f32[20]{0:T(128)S(1)} copy-done((f32[20]{0:T(128)S(1)}, f32[20]{0:T(128)}, u32[]{:S(2)}) %copy-start.3) | copy-done | bytes 104
  0.7 0.0 copy-start
  0.7 1.0 %copy-done = f32[1,40,24,128]{3,2,1,0:T(8,128)S(1)} copy-done((f32[1,40,24,128]{3,2,1,0:T(8,128)S(1)}, f32[1,40,24,128]{3,2,1,0:T(8,128)}, u32[]{:S(2)}) %copy-start) | copy-done | bytes 491544
  1.7 0.0 copy-start.1
  1.7 0.7 %copy-done.1 = s32[24,128]{1,0:T(8,128)S(1)} copy-done((s32[24,128]{1,0:T(8,128)S(1)}, s32[24,128]{1,0:T(8,128)}, u32[]{:S(2)}) %copy-start.1) | copy-done | bytes 12312
  2.4 0.0 copy-start.2
  2.4 0.7 %copy-done.2 = f32[20,20]{1,0:T(8,128)S(1)} copy-done((f32[20,20]{1,0:T(8,128)S(1)}, f32[20,20]{1,0:T(8,128)}, u32[]{:S(2)}) %copy-start.2) | copy-done | bytes 1624
  3.1 27.5 %shard_map.46 = f32[960,128]{1,0:T(8,128)S(1)} custom-call(f32[960,128]{1,0:T(8,128)S(1)} %bitcast.4, s32[24,128]{1,0:T(8,128)S(1)} %copy-done.1, f32[20,20]{1,0:T(8,128)S(1)} %copy-done.2, f32[1,20]{1,0:T(1,128)S(1)} %bitcast.5), custom_call_target="tpu_custom_call" | custom-call | flops 40000000 | bytes 983040 | tf_op jit(solution)/shard_map/pallas_call | solution.py:440
  30.6 0.8 %copy.6 = f32[1,40,24,128]{3,2,1,0:T(8,128)} copy(f32[1,40,24,128]{3,2,1,0:T(8,128)S(1)} %bitcast.3) | data formatting | bytes 983040
Async XLA Ops:
  0.0 0.7 %copy-start.3 = (f32[20]{0:T(128)S(1)}, f32[20]{0:T(128)}, u32[]{:S(2)}) copy-start(f32[20]{0:T(128)} %param.7) | copy-start | bytes 244
  0.7 1.0 %copy-start = (f32[1,40,24,128]{3,2,1,0:T(8,128)S(1)}, f32[1,40,24,128]{3,2,1,0:T(8,128)}, u32[]{:S(2)}) copy-start(f32[1,40,24,128]{3,2,1,0:T(8,128)} %param.4) | copy-start | bytes 1474564
  1.7 0.7 %copy-start.1 = (s32[24,128]{1,0:T(8,128)S(1)}, s32[24,128]{1,0:T(8,128)}, u32[]{:S(2)}) copy-start(s32[24,128]{1,0:T(8,128)} %depth.1) | copy-start | bytes 36868
  2.4 0.7 %copy-start.2 = (f32[20,20]{1,0:T(8,128)S(1)}, f32[20,20]{1,0:T(8,128)}, u32[]{:S(2)}) copy-start(f32[20,20]{1,0:T(8,128)} %rates.1) | copy-start | bytes 4804
